TPU v7x, 32 devices: a whole 2x2x4 slice. The times are simulated.
32 devices in a mesh: gx: 16 (over z, x, core), gy: 2 (over y).
Axes of the slice: x: 2, y: 2, z: 4, core: 2. Of those that a mesh axis runs over, the one named last changes fastest.
Arguments:
- density: float32 [128, 16, 256], P('gx', 'gy'), may hold values from 0.05 to 1
- passive: int32 [128, 16, 256], P('gx', 'gy'), may hold values 0 or 1
- fixed_nodes: int32 [128, 16, 256], P('gx', 'gy'), may hold values 0 or 1
- load_nodes: int32 [128, 16, 256], P('gx', 'gy'), may hold values 0 or 1
- port_load: float32 [3, 128, 16, 256], P(None, 'gx', 'gy'), may hold values from -12 to 12
- adjoint_guess: float32 [3, 128, 16, 256], P(None, 'gx', 'gy'), may hold values from -6 to 6
- primal: float32 [3, 128, 16, 256], P(None, 'gx', 'gy'), may hold values from -6 to 6
Outputs:
- sensitivity: float32 [128, 16, 256], P('gx', 'gy')
- adjoint: float32 [3, 128, 16, 256], P(None, 'gx', 'gy')
All inputs are finite; a program needn't handle non-finite values. No bound on the sum of `passive` or of `fixed_nodes` or of `load_nodes` on one device may be relied on, other than what follows from the above.
Results may differ from a plain program's by a relative error of at most 0.00013.
Values sent between devices are 32-bit elements; how exact they have to be, the bound alone decides.
A program may use at most 64 MiB of HBM per device.

v0:
```python
import math

import jax
import jax.numpy as jnp
import numpy as np
from jax import lax
from jax.sharding import PartitionSpec as P

ITERS = 2


EMIN = 0.01
BETA = 4.0
ETA = 0.5
RMIN = 3.0
HIGH = lax.Precision.HIGHEST


def with_halo(x, sides, width):
    for axis, dim in sides:
        size, length = (lax.axis_size(axis), x.shape[dim])
        up = [(i, (i + 1) % size) for i in range(size - 1)]
        down = [(j, i) for i, j in up]
        last = lax.slice_in_dim(x, length - width, length, axis=dim)
        first = lax.slice_in_dim(x, 0, width, axis=dim)
        before = lax.ppermute(last, axis, up)
        after = lax.ppermute(first, axis, down)
        x = jnp.concatenate([before, x, after], axis=dim)
    return x


def from_behind(x, axis, by):
    size = lax.axis_size(axis)
    pairs = [(i, i + by) for i in range(size) if 0 <= i + by < size]
    return lax.ppermute(x, axis, pairs)


def corner_list():
    return [
        (along_x, along_y, along_z)
        for along_x in (0, 1)
        for along_y in (0, 1)
        for along_z in (0, 1)
    ]


def element_matrix():
    poisson = 0.3
    lame = poisson / ((1 + poisson) * (1 - 2 * poisson))
    shear = 0.5 / (1 + poisson)
    elastic = np.zeros((6, 6))
    elastic[:3, :3] = lame
    for index in range(3):
        elastic[index, index] += 2 * shear
        elastic[index + 3, index + 3] = shear
    points = [0.5 - 0.5 / math.sqrt(3.0), 0.5 + 0.5 / math.sqrt(3.0)]
    result = np.zeros((24, 24))
    for point_s in points:
        for point_t in points:
            for point_r in points:
                strain = np.zeros((6, 24))
                for index, corner in enumerate(corner_list()):
                    factor_x = point_s if corner[0] else 1 - point_s
                    factor_y = point_t if corner[1] else 1 - point_t
                    factor_z = point_r if corner[2] else 1 - point_r
                    slope_x = (2 * corner[0] - 1) * factor_y * factor_z
                    slope_y = factor_x * (2 * corner[1] - 1) * factor_z
                    slope_z = factor_x * factor_y * (2 * corner[2] - 1)
                    column = 3 * index
                    strain[0, column] = slope_x
                    strain[1, column + 1] = slope_y
                    strain[2, column + 2] = slope_z
                    strain[3, column] = slope_y
                    strain[3, column + 1] = slope_x
                    strain[4, column + 1] = slope_z
                    strain[4, column + 2] = slope_y
                    strain[5, column] = slope_z
                    strain[5, column + 2] = slope_x
                result += 0.125 * strain.T @ elastic @ strain
    return result.astype(np.float32)


def diagonal_of(matrix):
    return np.array([matrix[index, index] for index in range(24)], dtype=np.float32)


def filter_offsets():
    found = []
    for shift_x in range(-2, 3):
        for shift_y in range(-2, 3):
            for shift_z in range(-2, 3):
                square = shift_x * shift_x + shift_y * shift_y + shift_z * shift_z
                if square < 9:
                    found.append((shift_x, shift_y, shift_z, RMIN - math.sqrt(square)))
    return found


def zshift(field, amount):
    if amount == 0:
        return field
    if amount > 0:
        zeros = jnp.zeros(field.shape[:-1] + (amount,), field.dtype)
        return jnp.concatenate([field[..., amount:], zeros], axis=-1)
    zeros = jnp.zeros(field.shape[:-1] + (-amount,), field.dtype)
    return jnp.concatenate([zeros, field[..., :amount]], axis=-1)


def filter_sum(padded, start, count_x, count_y):
    total = None
    for shift_x, shift_y, shift_z, weight in filter_offsets():
        piece = padded[
            start + shift_x : start + shift_x + count_x, start + shift_y : start + shift_y + count_y
        ]
        term = weight * zshift(piece, shift_z)
        total = term if total is None else total + term
    return total


def project(filtered):
    denom = 2.0 * math.tanh(BETA * ETA)
    bent = jnp.tanh(BETA * (filtered - ETA))
    return ((math.tanh(BETA * ETA) + bent) / denom, BETA * (1.0 - bent * bent) / denom)


def inside_mask(margin, count_x, count_y, count_z):
    first = (
        lax.axis_index("gx") * count_x - margin + jnp.arange(count_x + 2 * margin, dtype=jnp.int32)
    )
    second = (
        lax.axis_index("gy") * count_y - margin + jnp.arange(count_y + 2 * margin, dtype=jnp.int32)
    )
    inside_x = (first >= 0) & (first < lax.axis_size("gx") * count_x)
    inside_y = (second >= 0) & (second < lax.axis_size("gy") * count_y)
    plane = (inside_x[:, None] & inside_y[None, :]).astype(jnp.float32)
    return plane[:, :, None] * jnp.ones((1, 1, count_z), jnp.float32)


def corner_field(padded, corner, count_x, count_y, low):
    piece = padded[
        :, low + corner[0] : low + corner[0] + count_x, low + corner[1] : low + corner[1] + count_y
    ]
    return zshift(piece, corner[2])


def gather_corners(padded, count_x, count_y, low):
    return jnp.concatenate(
        [corner_field(padded, corner, count_x, count_y, low) for corner in corner_list()], axis=0
    )


def multiply_table(table, stacked):
    flat = stacked.reshape(24, -1)
    return jnp.dot(table, flat, precision=HIGH, preferred_element_type=jnp.float32).reshape(
        stacked.shape
    )


def assemble(forces, count_x, count_y):
    total = None
    for index, corner in enumerate(corner_list()):
        piece = forces[
            3 * index : 3 * index + 3,
            1 - corner[0] : 1 - corner[0] + count_x,
            1 - corner[1] : 1 - corner[1] + count_y,
        ]
        term = zshift(piece, -corner[2])
        total = term if total is None else total + term
    return total


def local(density, passive, fixed_nodes, load_nodes, port_load, adjoint_guess, primal):
    count_x, count_y, count_z = density.shape
    table = jnp.asarray(element_matrix())
    diagonal_table = jnp.asarray(diagonal_of(element_matrix()))
    free = (1 - fixed_nodes).astype(jnp.float32)
    solid = passive.astype(jnp.float32)
    blended = jnp.where(passive == 1, jnp.float32(1.0), density)
    blended_pad = with_halo(blended, (("gx", 0), ("gy", 1)), 2)
    weight_total = filter_sum(inside_mask(2, count_x, count_y, count_z), 2, count_x, count_y)
    filtered = filter_sum(blended_pad, 2, count_x, count_y) / weight_total
    heaviside, slope = project(filtered)
    physical = jnp.where(passive == 1, jnp.float32(1.0), heaviside)
    stiffness = EMIN + (1.0 - EMIN) * physical**3
    lower_rows = from_behind(stiffness[count_x - 1 : count_x], "gx", 1)
    stiff_rows_ext = jnp.concatenate([lower_rows, stiffness], axis=0)
    lower_columns = from_behind(stiff_rows_ext[:, count_y - 1 : count_y], "gy", 1)
    stiff_ext = jnp.concatenate([lower_columns, stiff_rows_ext], axis=1)
    diagonal = assemble(diagonal_table[:, None, None, None] * stiff_ext[None], count_x, count_y)
    inverse = free / diagonal

    def apply_padded(padded):
        forces = (
            multiply_table(table, gather_corners(padded, count_x + 1, count_y + 1, 0))
            * stiff_ext[None]
        )
        return free * assemble(forces, count_x, count_y)

    def operator(field):
        padded = with_halo(field, (("gx", 1), ("gy", 2)), 1)
        return (apply_padded(padded), padded)

    load_field = (free * load_nodes.astype(jnp.float32))[None] * port_load
    solution = free[None] * adjoint_guess
    masked_primal = free[None] * primal
    start_image, start_pad = operator(solution)
    residual = load_field - start_image
    precond = inverse * residual

    def inner_rz(first, second):
        return lax.psum(jnp.sum(first * second), ("gx", "gy"))

    direction = precond
    current = inner_rz(residual, precond)
    for step in range(ITERS):
        image, direction_pad = operator(direction)
        alpha = current / lax.psum(jnp.sum(direction * image), ("gx", "gy"))
        solution = solution + alpha * direction
        if step + 1 < ITERS:
            residual = residual - alpha * image
            precond = inverse * residual
            following = inner_rz(residual, precond)
            direction = precond + following / current * direction
            current = following
    upper_adjoint, upper_primal = from_behind((solution[:, :1], masked_primal[:, :1]), "gx", -1)
    adjoint_rows_ext = jnp.concatenate([solution, upper_adjoint], axis=1)
    primal_rows_ext = jnp.concatenate([masked_primal, upper_primal], axis=1)
    side_adjoint, side_primal = from_behind(
        (adjoint_rows_ext[:, :, :1], primal_rows_ext[:, :, :1]), "gy", -1
    )
    adjoint_view = jnp.concatenate([adjoint_rows_ext, side_adjoint], axis=2)
    primal_view = jnp.concatenate([primal_rows_ext, side_primal], axis=2)
    adjoint_low = 0
    primal_low = 0
    forces = multiply_table(table, gather_corners(primal_view, count_x, count_y, primal_low))
    energy = jnp.sum(gather_corners(adjoint_view, count_x, count_y, adjoint_low) * forces, axis=0)
    grad = -3.0 * (1.0 - EMIN) * physical**2 * energy * slope * (1.0 - solid)
    spread = grad / weight_total
    spread_pad = with_halo(spread, (("gx", 0), ("gy", 1)), 2)
    sensitivity = (1.0 - solid) * filter_sum(spread_pad, 2, count_x, count_y)
    return (sensitivity, solution)


def solution(mesh):
    in_specs = (
        P("gx", "gy", None),
        P("gx", "gy", None),
        P("gx", "gy", None),
        P("gx", "gy", None),
        P(None, "gx", "gy", None),
        P(None, "gx", "gy", None),
        P(None, "gx", "gy", None),
    )
    out_specs = (P("gx", "gy", None), P(None, "gx", "gy", None))
    return jax.shard_map(local, mesh=mesh, in_specs=in_specs, out_specs=out_specs, check_vma=False)
```

profile of v0, /device:TPU:5, one launch (start us, length us, event | category | flops | bytes accessed | tf_op | source)
XLA Modules:
  0.0 306.1 jit_solution(3942927103682816940)
XLA Ops:
  2.5 3.7 %collective-permute-start.4 = (f32[3,1,8,256]{3,2,1,0:T(8,128)S(1)}, f32[3,1,8,256]{3,2,1,0:T(8,128)S(1)}, u32[]{:S(2)}, u32[]{:S(2)}) collective-permute-start(f32[3,1,8,256]{3,2,1,0:T(8,128)S(1)} %get-tuple-element.109), channel_id=1, source_target_pairs={{0,2},{2,4},{4,6},{6,8},{8,10},{10,12},{12,14},{14,16},{16,18},{18... | collective-permute-start | bytes 73736 | tf_op jit(solution)/shard_map/ppermute | solution.py:26
  9.0 3.6 %collective-permute-start = (f32[2,8,256]{2,1,0:T(8,128)S(1)}, f32[2,8,256]{2,1,0:T(8,128)S(1)}, u32[]{:S(2)}, u32[]{:S(2)}) collective-permute-start(f32[2,8,256]{2,1,0:T(8,128)S(1)} %get-tuple-element.230), channel_id=1, source_target_pairs={{0,2},{2,4},{4,6},{6,8},{8,10},{10,12},{12,14},{14,16},{16,18},{18... | collective-permute-start | bytes 49160 | tf_op jit(solution)/shard_map/ppermute | solution.py:26
  19.0 4.0 %collective-permute-start.3 = (f32[12,2,256]{2,1,0:T(2,128)S(1)}, f32[12,2,256]{2,1,0:T(2,128)S(1)}, u32[]{:S(2)}, u32[]{:S(2)}) collective-permute-start(f32[12,2,256]{2,1,0:T(2,128)S(1)} %get-tuple-element.174), channel_id=1, source_target_pairs={{1,0},{3,2},{5,4},{7,6},{9,8},{11,10},{13,12},{15,14},{17,16},{19,... | collective-permute-start | bytes 73736 | tf_op jit(solution)/shard_map/ppermute | solution.py:27
  27.4 3.7 %fusion.28 = (f32[8,8,256]{2,1,0:T(8,128)S(1)}, f32[8,8,256]{2,1,0:T(8,128)}) fusion(s32[8,8,256]{2,1,0:T(8,128)S(1)} %copy-done.27, f32[8,8]{1,0:T(8,128)} %get-tuple-element.250, f32[8,8,255]{2,1,0:T(8,128)S(1)} %slice.1681, f32[8,8]{1,0:T(8,128)} %get-tuple-element.249, f32[8,8,254]{2,1,0:T(8,128)S(1)} %slice.1678, f32[8,8,255]{2,1,0:T(8,128)S(1)} %slice.1679, ...), kind=kLoop, calls=%fused_computation.183 | loop fusion | flops 5881856 | bytes 8130560 | tf_op jit(solution)/shard_map/add | solution.py:183
  31.5 4.8 %collective-permute-start.8 = (f32[1,8,256]{2,1,0:T(8,128)S(1)}, f32[1,8,256]{2,1,0:T(8,128)S(1)}, u32[]{:S(2)}, u32[]{:S(2)}) collective-permute-start(f32[1,8,256]{2,1,0:T(8,128)S(1)} %slice.2020), channel_id=1, source_target_pairs={{0,2},{2,4},{4,6},{6,8},{8,10},{10,12},{12,14},{14,16},{16,18},{18... | collective-permute-start | bytes 24584 | tf_op jit(solution)/shard_map/ppermute | solution.py:35
  37.6 4.0 %collective-permute-start.7 = (f32[3,10,1,256]{3,2,1,0:T(1,128)S(1)}, f32[3,10,1,256]{3,2,1,0:T(1,128)S(1)}, u32[]{:S(2)}, u32[]{:S(2)}) collective-permute-start(f32[3,10,1,256]{3,2,1,0:T(1,128)S(1)} %get-tuple-element.53), channel_id=1, source_target_pairs={{1,0},{3,2},{5,4},{7,6},{9,8},{11,10},{13,12},{15,14},{17,16},{19,... | collective-permute-start | bytes 92168 | tf_op jit(solution)/shard_map/ppermute | solution.py:27
  52.8 3.0 fusion.282
  60.8 3.0 collective-permute-start.10
  65.8 3.8 %collective-permute-done.11 = f32[3,1,8,256]{3,2,1,0:T(8,128)S(1)} collective-permute-done((f32[3,1,8,256]{3,2,1,0:T(8,128)S(1)}, f32[3,1,8,256]{3,2,1,0:T(8,128)S(1)}, u32[]{:S(2)}, u32[]{:S(2)}) %collective-permute-start.11) | collective-permute-done | bytes 24608 | tf_op jit(solution)/shard_map/ppermute | solution.py:27
  70.9 4.7 %collective-permute-start.13 = (f32[3,10,1,256]{3,2,1,0:T(1,128)S(1)}, f32[3,10,1,256]{3,2,1,0:T(1,128)S(1)}, u32[]{:S(2)}, u32[]{:S(2)}) collective-permute-start(f32[3,10,1,256]{3,2,1,0:T(1,128)S(1)} %get-tuple-element.49), channel_id=1, source_target_pairs={{1,0},{3,2},{5,4},{7,6},{9,8},{11,10},{13,12},{15,14},{17,16},{19,... | collective-permute-start | bytes 92168 | tf_op jit(solution)/shard_map/ppermute | solution.py:27
  85.8 3.0 fusion.283
  93.2 41.2 %all-reduce.240 = (f32[]{:T(128)}, f32[]{:T(128)}) all-reduce(f32[]{:T(128)} %get-tuple-element.3, f32[]{:T(128)} %get-tuple-element.2), channel_id=1, replica_groups=mesh['gx'=16,'gy'=2] {'gx','gy'}, use_global_device_ids=true, to_apply=%region_1.2 | all-reduce | flops 2 | bytes 16 | tf_op jit(solution)/shard_map/psum | solution.py:210
  136.7 41.9 %psum.30 = f32[]{:T(128)} all-reduce(f32[]{:T(128)} %multiply_reduce_fusion), channel_id=1, replica_groups=mesh['gx'=16,'gy'=2] {'gx','gy'}, use_global_device_ids=true, to_apply=%region_5.6 | all-reduce | flops 1 | bytes 8 | tf_op jit(solution)/shard_map/psum | solution.py:210
  180.4 2.9 collective-permute-start.20
  183.3 3.5 %collective-permute-start.14 = (f32[3,1,8,256]{3,2,1,0:T(8,128)S(1)}, f32[3,1,8,256]{3,2,1,0:T(8,128)S(1)}, u32[]{:S(2)}, u32[]{:S(2)}) collective-permute-start(f32[3,1,8,256]{3,2,1,0:T(8,128)S(1)} %get-tuple-element.105), channel_id=1, source_target_pairs={{0,2},{2,4},{4,6},{6,8},{8,10},{10,12},{12,14},{14,16},{16,18},{18... | collective-permute-start | bytes 73736 | tf_op jit(solution)/shard_map/ppermute | solution.py:26
  193.3 4.2 %collective-permute-start.17 = (f32[3,10,1,256]{3,2,1,0:T(1,128)S(1)}, f32[3,10,1,256]{3,2,1,0:T(1,128)S(1)}, u32[]{:S(2)}, u32[]{:S(2)}) collective-permute-start(f32[3,10,1,256]{3,2,1,0:T(1,128)S(1)} %get-tuple-element.45), channel_id=1, source_target_pairs={{1,0},{3,2},{5,4},{7,6},{9,8},{11,10},{13,12},{15,14},{17,16},{19,... | collective-permute-start | bytes 92168 | tf_op jit(solution)/shard_map/ppermute | solution.py:27
  207.6 3.0 fusion.284
  216.0 41.5 %psum.31 = f32[]{:T(128)} all-reduce(f32[]{:T(128)} %fusion.10), channel_id=1, replica_groups=mesh['gx'=16,'gy'=2] {'gx','gy'}, use_global_device_ids=true, to_apply=%region_7.8 | all-reduce | flops 1 | bytes 8 | tf_op jit(solution)/shard_map/psum | solution.py:216
  259.0 4.7 %collective-permute-start.18 = (f32[3,1,8,256]{3,2,1,0:T(8,128)S(1)}, f32[3,1,8,256]{3,2,1,0:T(8,128)S(1)}, u32[]{:S(2)}, u32[]{:S(2)}) collective-permute-start(f32[3,1,8,256]{3,2,1,0:T(8,128)S(1)} %slice.2074), channel_id=1, source_target_pairs={{2,0},{4,2},{6,4},{8,6},{10,8},{12,10},{14,12},{16,14},{18,16},{20... | collective-permute-start | bytes 73736 | tf_op jit(solution)/shard_map/ppermute | solution.py:35
  265.0 3.3 %collective-permute-start.19 = (f32[3,9,1,256]{3,2,1,0:T(1,128)S(1)}, f32[3,9,1,256]{3,2,1,0:T(1,128)S(1)}, u32[]{:S(2)}, u32[]{:S(2)}) collective-permute-start(f32[3,9,1,256]{3,2,1,0:T(1,128)S(1)} %pad_maximum_fusion.17), channel_id=1, source_target_pairs={{1,0},{3,2},{5,4},{7,6},{9,8},{11,10},{13,12},{15,14},{17,16},{19,... | collective-permute-start | bytes 82952 | tf_op jit(solution)/shard_map/ppermute | solution.py:35
  273.7 11.3 %concatenate.1075 = f32[24,16384]{1,0:T(8,128)S(1)} concatenate(f32[3,16384]{1,0:T(4,128)} %bitcast.46, f32[3,16384]{1,0:T(4,128)S(1)} %bitcast.45, f32[3,16384]{1,0:T(4,128)} %bitcast.52, f32[3,16384]{1,0:T(4,128)} %bitcast.49, f32[3,16384]{1,0:T(4,128)} %bitcast.47, f32[3,16384]{1,0:T(4,128)} %bitcast.48, f32[3,16384]{1,0:T(4,128)} %bitcast.51, f32[3,16384]{1,0:T(4,128)} %bitcast.50), dimensions={0} | concatenate | bytes 3145728 | tf_op jit(solution)/shard_map/concatenate | solution.py:146
  286.6 3.5 %fusion.26 = f32[8,8,256]{2,1,0:T(8,128)S(1)} fusion(f32[8,8,256]{2,1,0:T(8,128)S(1)} %reduce_sum.52, f32[8,8,256]{2,1,0:T(8,128)} %get-tuple-element.12, s32[8,8,256]{2,1,0:T(8,128)S(1)} %copy-done.28, f32[8,8]{1,0:T(8,128)} %get-tuple-element.250, f32[8,8,255]{2,1,0:T(8,128)} %copy-done.69, f32[8,8]{1,0:T(8,128)} %get-tuple-element.249, ...), kind=kLoop, calls=%fused_computation.181 | loop fusion | flops 2834432 | bytes 2484736 | tf_op jit(solution)/shard_map/div | solution.py:237
  294.4 2.9 collective-permute-done.23
  298.7 4.0 %collective-permute-start.25 = (f32[12,2,256]{2,1,0:T(2,128)S(1)}, f32[12,2,256]{2,1,0:T(2,128)S(1)}, u32[]{:S(2)}, u32[]{:S(2)}) collective-permute-start(f32[12,2,256]{2,1,0:T(2,128)S(1)} %get-tuple-element.170), channel_id=1, source_target_pairs={{1,0},{3,2},{5,4},{7,6},{9,8},{11,10},{13,12},{15,14},{17,16},{19,... | collective-permute-start | bytes 73736 | tf_op jit(solution)/shard_map/ppermute | solution.py:27
  (364 shorter events, 90.5 us)
Async XLA Ops:
  2.5 33.8 %collective-permute-start.4 = (f32[3,1,8,256]{3,2,1,0:T(8,128)S(1)}, f32[3,1,8,256]{3,2,1,0:T(8,128)S(1)}, u32[]{:S(2)}, u32[]{:S(2)}) collective-permute-start(f32[3,1,8,256]{3,2,1,0:T(8,128)S(1)} %get-tuple-element.109), channel_id=1, source_target_pairs={{0,2},{2,4},{4,6},{6,8},{8,10},{10,12},{12,14},{14,16},{16,18},{18... | collective-permute-start | bytes 73736 | tf_op jit(solution)/shard_map/ppermute | solution.py:26
  6.2 30.1 %collective-permute-start.5 = (f32[3,1,8,256]{3,2,1,0:T(8,128)S(1)}, f32[3,1,8,256]{3,2,1,0:T(8,128)S(1)}, u32[]{:S(2)}, u32[]{:S(2)}) collective-permute-start(f32[3,1,8,256]{3,2,1,0:T(8,128)S(1)} %get-tuple-element.110), channel_id=1, source_target_pairs={{2,0},{4,2},{6,4},{8,6},{10,8},{12,10},{14,12},{16,14},{18,16},{20... | collective-permute-start | bytes 73736 | tf_op jit(solution)/shard_map/ppermute | solution.py:27
  9.0 8.7 %collective-permute-start = (f32[2,8,256]{2,1,0:T(8,128)S(1)}, f32[2,8,256]{2,1,0:T(8,128)S(1)}, u32[]{:S(2)}, u32[]{:S(2)}) collective-permute-start(f32[2,8,256]{2,1,0:T(8,128)S(1)} %get-tuple-element.230), channel_id=1, source_target_pairs={{0,2},{2,4},{4,6},{6,8},{8,10},{10,12},{12,14},{14,16},{16,18},{18... | collective-permute-start | bytes 49160 | tf_op jit(solution)/shard_map/ppermute | solution.py:26
  12.6 5.1 %collective-permute-start.1 = (f32[2,8,256]{2,1,0:T(8,128)S(1)}, f32[2,8,256]{2,1,0:T(8,128)S(1)}, u32[]{:S(2)}, u32[]{:S(2)}) collective-permute-start(f32[2,8,256]{2,1,0:T(8,128)S(1)} %get-tuple-element.231), channel_id=1, source_target_pairs={{2,0},{4,2},{6,4},{8,6},{10,8},{12,10},{14,12},{16,14},{18,16},{20... | collective-permute-start | bytes 49160 | tf_op jit(solution)/shard_map/ppermute | solution.py:27
  17.7 5.6 %collective-permute-start.2 = (f32[12,2,256]{2,1,0:T(2,128)S(1)}, f32[12,2,256]{2,1,0:T(2,128)S(1)}, u32[]{:S(2)}, u32[]{:S(2)}) collective-permute-start(f32[12,2,256]{2,1,0:T(2,128)S(1)} %get-tuple-element.173), channel_id=1, source_target_pairs={{0,1},{2,3},{4,5},{6,7},{8,9},{10,11},{12,13},{14,15},{16,17},{18,... | collective-permute-start | bytes 73736 | tf_op jit(solution)/shard_map/ppermute | solution.py:26
  19.0 4.9 %collective-permute-start.3 = (f32[12,2,256]{2,1,0:T(2,128)S(1)}, f32[12,2,256]{2,1,0:T(2,128)S(1)}, u32[]{:S(2)}, u32[]{:S(2)}) collective-permute-start(f32[12,2,256]{2,1,0:T(2,128)S(1)} %get-tuple-element.174), channel_id=1, source_target_pairs={{1,0},{3,2},{5,4},{7,6},{9,8},{11,10},{13,12},{15,14},{17,16},{19,... | collective-permute-start | bytes 73736 | tf_op jit(solution)/shard_map/ppermute | solution.py:27
  31.5 10.1 %collective-permute-start.8 = (f32[1,8,256]{2,1,0:T(8,128)S(1)}, f32[1,8,256]{2,1,0:T(8,128)S(1)}, u32[]{:S(2)}, u32[]{:S(2)}) collective-permute-start(f32[1,8,256]{2,1,0:T(8,128)S(1)} %slice.2020), channel_id=1, source_target_pairs={{0,2},{2,4},{4,6},{6,8},{8,10},{10,12},{12,14},{14,16},{16,18},{18... | collective-permute-start | bytes 24584 | tf_op jit(solution)/shard_map/ppermute | solution.py:35
  36.3 7.2 %collective-permute-start.6 = (f32[3,10,1,256]{3,2,1,0:T(1,128)S(1)}, f32[3,10,1,256]{3,2,1,0:T(1,128)S(1)}, u32[]{:S(2)}, u32[]{:S(2)}) collective-permute-start(f32[3,10,1,256]{3,2,1,0:T(1,128)S(1)} %get-tuple-element.54), channel_id=1, source_target_pairs={{0,1},{2,3},{4,5},{6,7},{8,9},{10,11},{12,13},{14,15},{16,17},{18,... | collective-permute-start | bytes 92168 | tf_op jit(solution)/shard_map/ppermute | solution.py:26
  37.6 5.9 %collective-permute-start.7 = (f32[3,10,1,256]{3,2,1,0:T(1,128)S(1)}, f32[3,10,1,256]{3,2,1,0:T(1,128)S(1)}, u32[]{:S(2)}, u32[]{:S(2)}) collective-permute-start(f32[3,10,1,256]{3,2,1,0:T(1,128)S(1)} %get-tuple-element.53), channel_id=1, source_target_pairs={{1,0},{3,2},{5,4},{7,6},{9,8},{11,10},{13,12},{15,14},{17,16},{19,... | collective-permute-start | bytes 92168 | tf_op jit(solution)/shard_map/ppermute | solution.py:27
  42.2 15.3 %collective-permute-start.9 = (f32[9,1,256]{2,1,0:T(1,128)}, f32[9,1,256]{2,1,0:T(1,128)}, u32[]{:S(2)}, u32[]{:S(2)}) collective-permute-start(f32[9,1,256]{2,1,0:T(1,128)} %pad_maximum_fusion.24), channel_id=1, source_target_pairs={{0,1},{2,3},{4,5},{6,7},{8,9},{10,11},{12,13},{14,15},{16,17},{18,... | collective-permute-start | bytes 27656 | tf_op jit(solution)/shard_map/ppermute | solution.py:35
  60.8 5.0 %collective-permute-start.10 = (f32[3,1,8,256]{3,2,1,0:T(8,128)S(1)}, f32[3,1,8,256]{3,2,1,0:T(8,128)S(1)}, u32[]{:S(2)}, u32[]{:S(2)}) collective-permute-start(f32[3,1,8,256]{3,2,1,0:T(8,128)S(1)} %get-tuple-element.107), channel_id=1, source_target_pairs={{0,2},{2,4},{4,6},{6,8},{8,10},{10,12},{12,14},{14,16},{16,18},{18... | collective-permute-start | bytes 73736 | tf_op jit(solution)/shard_map/ppermute | solution.py:26
  63.9 5.7 %collective-permute-start.11 = (f32[3,1,8,256]{3,2,1,0:T(8,128)S(1)}, f32[3,1,8,256]{3,2,1,0:T(8,128)S(1)}, u32[]{:S(2)}, u32[]{:S(2)}) collective-permute-start(f32[3,1,8,256]{3,2,1,0:T(8,128)S(1)} %get-tuple-element.108), channel_id=1, source_target_pairs={{2,0},{4,2},{6,4},{8,6},{10,8},{12,10},{14,12},{16,14},{18,16},{20... | collective-permute-start | bytes 73736 | tf_op jit(solution)/shard_map/ppermute | solution.py:27
  69.6 6.0 %collective-permute-start.12 = (f32[3,10,1,256]{3,2,1,0:T(1,128)S(1)}, f32[3,10,1,256]{3,2,1,0:T(1,128)S(1)}, u32[]{:S(2)}, u32[]{:S(2)}) collective-permute-start(f32[3,10,1,256]{3,2,1,0:T(1,128)S(1)} %get-tuple-element.50), channel_id=1, source_target_pairs={{0,1},{2,3},{4,5},{6,7},{8,9},{10,11},{12,13},{14,15},{16,17},{18,... | collective-permute-start | bytes 92168 | tf_op jit(solution)/shard_map/ppermute | solution.py:26
  70.9 5.5 %collective-permute-start.13 = (f32[3,10,1,256]{3,2,1,0:T(1,128)S(1)}, f32[3,10,1,256]{3,2,1,0:T(1,128)S(1)}, u32[]{:S(2)}, u32[]{:S(2)}) collective-permute-start(f32[3,10,1,256]{3,2,1,0:T(1,128)S(1)} %get-tuple-element.49), channel_id=1, source_target_pairs={{1,0},{3,2},{5,4},{7,6},{9,8},{11,10},{13,12},{15,14},{17,16},{19,... | collective-permute-start | bytes 92168 | tf_op jit(solution)/shard_map/ppermute | solution.py:27
  180.4 8.4 %collective-permute-start.20 = (f32[3,1,8,256]{3,2,1,0:T(8,128)S(1)}, f32[3,1,8,256]{3,2,1,0:T(8,128)S(1)}, u32[]{:S(2)}, u32[]{:S(2)}) collective-permute-start(f32[3,1,8,256]{3,2,1,0:T(8,128)S(1)} %slice.2082), channel_id=1, source_target_pairs={{2,0},{4,2},{6,4},{8,6},{10,8},{12,10},{14,12},{16,14},{18,16},{20... | collective-permute-start | bytes 73736 | tf_op jit(solution)/shard_map/ppermute | solution.py:35
  183.3 7.0 %collective-permute-start.14 = (f32[3,1,8,256]{3,2,1,0:T(8,128)S(1)}, f32[3,1,8,256]{3,2,1,0:T(8,128)S(1)}, u32[]{:S(2)}, u32[]{:S(2)}) collective-permute-start(f32[3,1,8,256]{3,2,1,0:T(8,128)S(1)} %get-tuple-element.105), channel_id=1, source_target_pairs={{0,2},{2,4},{4,6},{6,8},{8,10},{10,12},{12,14},{14,16},{16,18},{18... | collective-permute-start | bytes 73736 | tf_op jit(solution)/shard_map/ppermute | solution.py:26
  186.8 5.1 %collective-permute-start.15 = (f32[3,1,8,256]{3,2,1,0:T(8,128)S(1)}, f32[3,1,8,256]{3,2,1,0:T(8,128)S(1)}, u32[]{:S(2)}, u32[]{:S(2)}) collective-permute-start(f32[3,1,8,256]{3,2,1,0:T(8,128)S(1)} %get-tuple-element.106), channel_id=1, source_target_pairs={{2,0},{4,2},{6,4},{8,6},{10,8},{12,10},{14,12},{16,14},{18,16},{20... | collective-permute-start | bytes 73736 | tf_op jit(solution)/shard_map/ppermute | solution.py:27
  188.8 8.7 %collective-permute-start.21 = (f32[3,9,1,256]{3,2,1,0:T(1,128)S(1)}, f32[3,9,1,256]{3,2,1,0:T(1,128)S(1)}, u32[]{:S(2)}, u32[]{:S(2)}) collective-permute-start(f32[3,9,1,256]{3,2,1,0:T(1,128)S(1)} %pad_maximum_fusion.16), channel_id=1, source_target_pairs={{1,0},{3,2},{5,4},{7,6},{9,8},{11,10},{13,12},{15,14},{17,16},{19,... | collective-permute-start | bytes 82952 | tf_op jit(solution)/shard_map/ppermute | solution.py:35
  192.0 6.0 %collective-permute-start.16 = (f32[3,10,1,256]{3,2,1,0:T(1,128)S(1)}, f32[3,10,1,256]{3,2,1,0:T(1,128)S(1)}, u32[]{:S(2)}, u32[]{:S(2)}) collective-permute-start(f32[3,10,1,256]{3,2,1,0:T(1,128)S(1)} %get-tuple-element.46), channel_id=1, source_target_pairs={{0,1},{2,3},{4,5},{6,7},{8,9},{10,11},{12,13},{14,15},{16,17},{18,... | collective-permute-start | bytes 92168 | tf_op jit(solution)/shard_map/ppermute | solution.py:26
  193.3 5.0 %collective-permute-start.17 = (f32[3,10,1,256]{3,2,1,0:T(1,128)S(1)}, f32[3,10,1,256]{3,2,1,0:T(1,128)S(1)}, u32[]{:S(2)}, u32[]{:S(2)}) collective-permute-start(f32[3,10,1,256]{3,2,1,0:T(1,128)S(1)} %get-tuple-element.45), channel_id=1, source_target_pairs={{1,0},{3,2},{5,4},{7,6},{9,8},{11,10},{13,12},{15,14},{17,16},{19,... | collective-permute-start | bytes 92168 | tf_op jit(solution)/shard_map/ppermute | solution.py:27
  259.0 6.0 %collective-permute-start.18 = (f32[3,1,8,256]{3,2,1,0:T(8,128)S(1)}, f32[3,1,8,256]{3,2,1,0:T(8,128)S(1)}, u32[]{:S(2)}, u32[]{:S(2)}) collective-permute-start(f32[3,1,8,256]{3,2,1,0:T(8,128)S(1)} %slice.2074), channel_id=1, source_target_pairs={{2,0},{4,2},{6,4},{8,6},{10,8},{12,10},{14,12},{16,14},{18,16},{20... | collective-permute-start | bytes 73736 | tf_op jit(solution)/shard_map/ppermute | solution.py:35
  265.0 5.1 %collective-permute-start.19 = (f32[3,9,1,256]{3,2,1,0:T(1,128)S(1)}, f32[3,9,1,256]{3,2,1,0:T(1,128)S(1)}, u32[]{:S(2)}, u32[]{:S(2)}) collective-permute-start(f32[3,9,1,256]{3,2,1,0:T(1,128)S(1)} %pad_maximum_fusion.17), channel_id=1, source_target_pairs={{1,0},{3,2},{5,4},{7,6},{9,8},{11,10},{13,12},{15,14},{17,16},{19,... | collective-permute-start | bytes 82952 | tf_op jit(solution)/shard_map/ppermute | solution.py:35
  292.3 5.1 %collective-permute-start.23 = (f32[2,8,256]{2,1,0:T(8,128)S(1)}, f32[2,8,256]{2,1,0:T(8,128)S(1)}, u32[]{:S(2)}, u32[]{:S(2)}) collective-permute-start(f32[2,8,256]{2,1,0:T(8,128)S(1)} %get-tuple-element.217), channel_id=1, source_target_pairs={{2,0},{4,2},{6,4},{8,6},{10,8},{12,10},{14,12},{16,14},{18,16},{20... | collective-permute-start | bytes 49160 | tf_op jit(solution)/shard_map/ppermute | solution.py:27
  297.4 5.6 %collective-permute-start.24 = (f32[12,2,256]{2,1,0:T(2,128)S(1)}, f32[12,2,256]{2,1,0:T(2,128)S(1)}, u32[]{:S(2)}, u32[]{:S(2)}) collective-permute-start(f32[12,2,256]{2,1,0:T(2,128)S(1)} %get-tuple-element.169), channel_id=1, source_target_pairs={{0,1},{2,3},{4,5},{6,7},{8,9},{10,11},{12,13},{14,15},{16,17},{18,... | collective-permute-start | bytes 73736 | tf_op jit(solution)/shard_map/ppermute | solution.py:26
  (86 other events, 1242.5 us)
where the time goes:
time: 310 us; the launch traced here: 306 us
  blocking collectives  125 us (40%)
  starting transfers between devices  71.6 us (23%)
  local copies, waits for them, and re-layouts  56.7 us (18%)
  other arithmetic  25.3 us (8%)
  waiting for transfers between devices  11 us (4%)
  matrix products  10.5 us (3%)
  between operations  6.45 us (2%)
    psum x2, blocking collectives, inner_rz(): return lax.psum(jnp.sum(first * second), ('gx', 'gy'))  83.1 us
    psum x1, blocking collectives, local(): alpha = current / lax.psum(jnp.sum(direction * image), ('gx', 'gy'))  41.5 us
    ppermute x10, starting transfers between devices, with_halo(): after = lax.ppermute(first, axis, down)  30.7 us
    unnamed x206, local copies, waits for them, and re-layouts  24.7 us
    ppermute x10, starting transfers between devices, with_halo(): before = lax.ppermute(last, axis, up)  22.5 us
    ppermute x6, starting transfers between devices, from_behind(): return lax.ppermute(x, axis, pairs)  18.5 us
    concatenate x5, local copies, waits for them, and re-layouts, gather_corners(): jnp.concatenate([corner_field(padded, corner, count_x, count_y, low) for...  13.7 us
    ppermute x10, waiting for transfers between devices, with_halo(): after = lax.ppermute(first, axis, down)  10.7 us
  transfers between devices with their start and end apart: 26, of which 8 were waited for; matrix products, arithmetic and copies ran while one was open for 10% of the time, Pallas kernels for 0%

commit v1 on v0

v1 whole, which is shorter than its diff:
```python
import math

import jax
import jax.numpy as jnp
import numpy as np
from jax import lax
from jax.experimental import pallas as pl
from jax.experimental.pallas import tpu as pltpu
from jax.sharding import PartitionSpec as P

EMIN = 0.01
BETA = 4.0
ETA = 0.5
RMIN = 3.0
N = 8
W = 4
L = N + 2 * W
NZ = 256
MESH = pl.DeviceIdType.MESH


def corner_list():
    return [
        (along_x, along_y, along_z)
        for along_x in (0, 1)
        for along_y in (0, 1)
        for along_z in (0, 1)
    ]


def element_matrix():
    poisson = 0.3
    lame = poisson / ((1 + poisson) * (1 - 2 * poisson))
    shear = 0.5 / (1 + poisson)
    elastic = np.zeros((6, 6))
    elastic[:3, :3] = lame
    for index in range(3):
        elastic[index, index] += 2 * shear
        elastic[index + 3, index + 3] = shear
    points = [0.5 - 0.5 / math.sqrt(3.0), 0.5 + 0.5 / math.sqrt(3.0)]
    result = np.zeros((24, 24))
    for point_s in points:
        for point_t in points:
            for point_r in points:
                strain = np.zeros((6, 24))
                for index, corner in enumerate(corner_list()):
                    factor_x = point_s if corner[0] else 1 - point_s
                    factor_y = point_t if corner[1] else 1 - point_t
                    factor_z = point_r if corner[2] else 1 - point_r
                    slope_x = (2 * corner[0] - 1) * factor_y * factor_z
                    slope_y = factor_x * (2 * corner[1] - 1) * factor_z
                    slope_z = factor_x * factor_y * (2 * corner[2] - 1)
                    column = 3 * index
                    strain[0, column] = slope_x
                    strain[1, column + 1] = slope_y
                    strain[2, column + 2] = slope_z
                    strain[3, column] = slope_y
                    strain[3, column + 1] = slope_x
                    strain[4, column + 1] = slope_z
                    strain[4, column + 2] = slope_y
                    strain[5, column] = slope_z
                    strain[5, column + 2] = slope_x
                result += 0.125 * strain.T @ elastic @ strain
    return result


def modal_matrix():
    pair = np.array([[1.0, 1.0], [-1.0, 1.0]])
    change = np.kron(np.kron(np.kron(pair, pair), pair), np.eye(3))
    back = np.linalg.inv(change)
    modal = back.T @ element_matrix() @ back
    rows = []
    for row in range(24):
        rows.append([(col, float(modal[row, col])) for col in range(24) if abs(modal[row, col]) > 1e-9])
    return rows


MODAL = modal_matrix()
DIAG = float(element_matrix()[0, 0])

DEN, PAS, FR, U, LD, PR = 0, 1, 2, 3, 6, 9
FIELDS = 12

MSG = {
    (0, 1): [(DEN, -4, 4), (PAS, -2, 2), (FR, -1, 1), (LD, -1, 1)],
    (0, -1): [(DEN, N, 4), (PAS, N, 2), (FR, N, 2)],
    (1, 1): [(U + c, -2, 2) for c in range(3)] + [(LD + 1, -1, 1), (LD + 2, -1, 1)],
    (1, -1): [(U + c, N, 3) for c in range(3)] + [(LD + c, N, 2) for c in range(3)],
    (2, -1): [(PR + c, N, 1) for c in range(3)],
    (3, 1): [(c, -2, 2) for c in range(3)],
    (3, -1): [(c, N, 2) for c in range(3)],
}
DIAG_ROWS = {
    (0, 1): (4, 4), (0, -1): (0, 4),
    (1, 1): (6, 2), (1, -1): (0, 3),
    (2, -1): (0, 1),
    (3, 1): (6, 2), (3, -1): (0, 2),
}


def units(msg, way):
    return sum(count for _, _, count in MSG[msg, way])


def pad8(count):
    return (count + 7) // 8 * 8


def routes():
    found = []
    for msg in range(4):
        for dx in (-1, 0, 1):
            for dy in (-1, 0, 1):
                if (dx, dy) == (0, 0):
                    continue
                if (dx and (msg, dx) not in MSG) or (dy and (msg, dy) not in MSG):
                    continue
                found.append((msg, dx, dy))
    return found


ROUTES = routes()
STAGES = [(msg, axis, way) for (msg, way) in MSG for axis in (0, 1)]


def stage_shape(msg, axis, way):
    if axis == 0:
        return (units(msg, way), N, NZ)
    return (N, pad8(units(msg, way)), NZ)


def route_shape(msg, dx, dy):
    if dy == 0:
        return stage_shape(msg, 0, dx)
    if dx == 0:
        return stage_shape(msg, 1, dy)
    return (DIAG_ROWS[msg, dx][1], pad8(units(msg, dy)), NZ)


def zshift(value, amount):
    lane = lax.broadcasted_iota(jnp.int32, value.shape, value.ndim - 1)
    moved = pltpu.roll(value, (-amount) % NZ, value.ndim - 1)
    keep = (lane < NZ - amount) if amount > 0 else (lane >= -amount)
    return jnp.where(keep, moved, 0.0)


def yshift(value, amount):
    return pltpu.roll(value, (-amount) % value.shape[-2], value.ndim - 2)


def filter_row(rows):
    across = [rows[2], rows[1] + rows[3], rows[0] + rows[4]]
    total = None
    for dz in range(3):
        plane = None
        for dy in range(3):
            part = None
            for dx in range(3):
                square = dx * dx + dy * dy + dz * dz
                if square < 9:
                    term = (RMIN - math.sqrt(square)) * across[dx]
                    part = term if part is None else part + term
            if part is None:
                continue
            if dy:
                part = yshift(part, dy) + yshift(part, -dy)
            plane = part if plane is None else plane + part
        if dz:
            plane = zshift(plane, dz) + zshift(plane, -dz)
        total = plane if total is None else total + plane
    return total


def transform(value):
    up = zshift(value, 1)
    out = [value + up, up - value]
    ups = [yshift(v, 1) for v in out]
    return [out[0] + ups[0], out[1] + ups[1], ups[0] - out[0], ups[1] - out[1]]


def put_transform(held, row, values):
    for c in range(3):
        for k, value in enumerate(transform(values[c])):
            held[4 * c + k, row] = value


def modes(held, row, part=slice(None)):
    out = [None] * 24
    for c in range(3):
        for k in range(4):
            low, high = held[4 * c + k, row, part, :], held[4 * c + k, row + 1, part, :]
            out[3 * k + c] = low + high
            out[12 + 3 * k + c] = high - low
    return out


def stress(mode):
    out = []
    for row in MODAL:
        total = None
        for col, weight in row:
            term = weight * mode[col]
            total = term if total is None else total + term
        out.append(total)
    return out


def dot_modes(first, second):
    total = None
    for a, b in zip(first, second):
        if b is not None:
            total = a * b if total is None else total + a * b
    return total


def spread_forces(held, work, stiff, low, high):
    for k in range(12):
        work[k, low] = jnp.zeros((L, NZ), jnp.float32)

    def step(row, carry):
        scale = stiff[row]
        force = stress(modes(held, row))
        for c in range(3):
            for k in range(4):
                even, odd = force[3 * k + c], force[12 + 3 * k + c]
                odd = odd * scale
                slot = 4 * c + k
                if even is None:
                    work[slot, row] = work[slot, row] - odd
                    work[slot, row + 1] = odd
                else:
                    even = even * scale
                    work[slot, row] = work[slot, row] + (even - odd)
                    work[slot, row + 1] = even + odd
        return carry

    lax.fori_loop(low, high, step, 0)


def node_forces(work, row, c):
    out = []
    for z in range(2):
        even, odd = work[4 * c + z, row], work[4 * c + 2 + z, row]
        out.append((even - odd) + yshift(even + odd, -1))
    return (out[0] - out[1]) + zshift(out[0] + out[1], -1)


def kernel(size_x, size_y, *refs):
    inputs, refs = refs[:7], refs[7:]
    density, passive, fixed, load_nodes, port, guess, primal = inputs
    (sens, adjoint), refs = refs[:2], refs[2:]
    stages, refs = dict(zip(STAGES, refs)), refs[len(STAGES):]
    lands, refs = dict(zip(ROUTES, refs)), refs[len(ROUTES):]
    (ext, mask, weight, phys, slope, stiff, factor, res_z, q, inv, tu, td, tq, tp, work, sp,
     red1, red2, acc, send_sem, recv_sem, red_send, red_recv) = refs
    gx, gy = lax.axis_index("gx"), lax.axis_index("gy")
    lower = 4
    upper = size_x // lower * size_y
    group, rank = gx // lower, gx % lower
    upper_rank = group * size_y + gy

    def there(dx, dy):
        ok = None
        for pos, size, d in ((gx, size_x, dx), (gy, size_y, dy)):
            if d:
                this = (pos + d >= 0) & (pos + d < size)
                ok = this if ok is None else ok & this
        return ok

    def peer1(k):
        return (group * lower + (rank + k) % lower, gy)

    def peer2(k):
        other = (upper_rank + k) % upper
        return ((other // size_y) * lower + rank, other % size_y)

    barrier = pltpu.get_barrier_semaphore()
    expected = jnp.int32(lower - 1 + upper - 1)
    for dx in (-1, 0, 1):
        for dy in (-1, 0, 1):
            if (dx, dy) != (0, 0):
                ok = there(dx, dy)
                expected = expected + ok.astype(jnp.int32)

                @pl.when(ok)
                def _():
                    pl.semaphore_signal(barrier, inc=1, device_id=(gx + dx, gy + dy), device_id_type=MESH)
    for k in range(1, lower):
        pl.semaphore_signal(barrier, inc=1, device_id=peer1(k), device_id_type=MESH)
    for k in range(1, upper):
        pl.semaphore_signal(barrier, inc=1, device_id=peer2(k), device_id_type=MESH)

    own = slice(W, W + N)
    for f in range(FIELDS):
        def clear(i, carry):
            ext[f, i] = jnp.zeros((L, NZ), jnp.float32)
            return carry
        lax.fori_loop(0, L, clear, 0)

    def fill(i, carry):
        free = (1 - fixed[i]).astype(jnp.float32)
        solid = passive[i] == 1
        loaded = free * load_nodes[i].astype(jnp.float32)
        ext[DEN, W + i, own, :] = jnp.where(solid, 1.0, density[i])
        ext[PAS, W + i, own, :] = passive[i].astype(jnp.float32)
        ext[FR, W + i, own, :] = free
        for c in range(3):
            ext[U + c, W + i, own, :] = free * guess[c, i]
            ext[LD + c, W + i, own, :] = loaded * port[c, i]
            ext[PR + c, W + i, own, :] = free * primal[c, i]
        return carry

    lax.fori_loop(0, N, fill, 0)

    def pack(msg, source):
        for way in (1, -1):
            if (msg, way) not in MSG:
                continue
            flat_x, flat_y = stages[msg, 0, way], stages[msg, 1, way]
            at = 0
            for f, first, count in MSG[msg, way]:
                start = W + (first + N if way == 1 else first - N)
                flat_x[at:at + count] = source[f, start:start + count, own, :]
                flat_y[:, at:at + count, :] = source[f, own, start:start + count, :]
                at += count
            if at < flat_y.shape[1]:
                flat_y[:, at:, :] = jnp.zeros((N, flat_y.shape[1] - at, NZ), jnp.float32)

    def copy(route):
        msg, dx, dy = route
        at = ROUTES.index(route)
        if dy == 0:
            source = stages[msg, 0, dx]
        elif dx == 0:
            source = stages[msg, 1, dy]
        else:
            first, count = DIAG_ROWS[msg, dx]
            source = stages[msg, 1, dy].at[first:first + count]
        return pltpu.make_async_remote_copy(
            src_ref=source,
            dst_ref=lands[route],
            send_sem=send_sem.at[at],
            recv_sem=recv_sem.at[at],
            device_id=(gx + dx, gy + dy),
            device_id_type=MESH,
        )

    def send(msg):
        for route in ROUTES:
            if route[0] == msg:
                @pl.when(there(route[1], route[2]))
                def _():
                    copy(route).start()

    def receive(msg, target):
        for route in ROUTES:
            if route[0] != msg:
                continue
            _, dx, dy = route

            @pl.when(there(-dx, -dy))
            def _():
                copy(route).wait_recv()
                land = lands[route]
                at = 0
                for f, first, count in MSG[msg, dy if dy else dx]:
                    begin = W + first
                    if dy == 0:
                        target[f, begin:begin + count, own, :] = land[at:at + count]
                    elif dx == 0:
                        target[f, own, begin:begin + count, :] = land[:, at:at + count, :]
                    else:
                        source, rows = DIAG_ROWS[msg, dx]
                        row = W + (source - N if dx == 1 else source + N)
                        target[f, row:row + rows, begin:begin + count, :] = land[:, at:at + count, :]
                    at += count

    def finish(msg):
        for route in ROUTES:
            if route[0] == msg:
                @pl.when(there(route[1], route[2]))
                def _():
                    copy(route).wait_send()

    pack(0, ext)
    pl.semaphore_wait(barrier, expected)
    send(0)
    pack(1, ext)
    send(1)
    pack(2, ext)
    send(2)

    sub = lax.broadcasted_iota(jnp.int32, (L, NZ), 0)
    at_y = gy * N - W + sub
    inside_y = ((at_y >= 0) & (at_y < size_y * N)).astype(jnp.float32)
    owned = ((sub >= W) & (sub < W + N)).astype(jnp.float32)

    def inside_x(i):
        at_x = gx * N - W + i
        return ((at_x >= 0) & (at_x < size_x * N)).astype(jnp.float32)

    def weigh(i, carry):
        total = filter_row([inside_x(i + d) * inside_y for d in range(-2, 3)])
        weight[i] = 1.0 / jnp.where(total > 0.0, total, 1.0)
        return carry

    lax.fori_loop(2, 14, weigh, 0)

    receive(0, ext)
    denom = 2.0 * math.tanh(BETA * ETA)

    def densities(i, carry):
        filtered = filter_row([ext[DEN, i + d] for d in range(-2, 3)]) * weight[i]
        bent = jnp.tanh(BETA * (filtered - ETA))
        solid = ext[PAS, i]
        physical = jnp.where(solid == 1.0, 1.0, (math.tanh(BETA * ETA) + bent) / denom)
        square = physical * physical
        stiff[i] = (EMIN + (1.0 - EMIN) * (square * physical)) * (inside_x(i) * inside_y)
        gain = BETA * (1.0 - bent * bent) / denom
        factor[i] = (-3.0 * (1.0 - EMIN)) * square * gain * (1.0 - solid) * weight[i]
        return carry

    lax.fori_loop(2, 14, densities, 0)

    receive(1, ext)

    def load_u(i, carry):
        put_transform(tu, i, [ext[U + c, i] for c in range(3)])
        return carry

    lax.fori_loop(2, 15, load_u, 0)
    spread_forces(tu, work, stiff, 2, 14)
    acc[...] = jnp.zeros_like(acc)

    def is_owned(i):
        return ((i >= W) & (i < W + N)).astype(jnp.float32) * owned

    def residuals(i, carry):
        free = ext[FR, i]
        pair = stiff[i] + stiff[i - 1]
        pair = pair + yshift(pair, -1)
        total = DIAG * (pair + zshift(pair, -1))
        inverse = free / jnp.where(total > 0.0, total, 1.0)
        inv[i] = inverse
        dot = None
        values = []
        for c in range(3):
            residual = ext[LD + c, i] - free * node_forces(work, i, c)
            value = inverse * residual
            res_z[c, i] = value
            values.append(value)
            dot = residual * value if dot is None else dot + residual * value
        put_transform(td, i, values)
        acc[0] = acc[0] + is_owned(i) * dot
        return carry

    lax.fori_loop(3, 14, residuals, 0)
    spread_forces(td, work, stiff, 3, 13)

    def images(i, carry):
        free, inverse = ext[FR, i], inv[i]
        dot_w = dot_q = None
        values = []
        for c in range(3):
            image = free * node_forces(work, i, c)
            value = inverse * image
            q[c, i] = value
            values.append(value)
            first, second = image * res_z[c, i], image * value
            dot_w = first if dot_w is None else dot_w + first
            dot_q = second if dot_q is None else dot_q + second
        put_transform(tq, i, values)
        acc[1] = acc[1] + is_owned(i) * dot_w
        acc[2] = acc[2] + is_owned(i) * dot_q
        return carry

    lax.fori_loop(4, 13, images, 0)

    def curvature(i, total):
        mode = modes(tq, i, own)
        return total + stiff[i, own, :] * dot_modes(mode, stress(mode))

    last = lax.fori_loop(W, W + N, curvature, jnp.zeros((N, NZ), jnp.float32))

    parts = []
    for value in (acc[0], acc[1], acc[2], last):
        line = jnp.sum(value, axis=0, keepdims=True)
        parts.append(line[:, :128] + line[:, 128:])
    for k, part in enumerate(parts):
        red1[0, k:k + 1, :] = part
    red1[0, 4:8, :] = jnp.zeros((4, 128), jnp.float32)

    def reduce_copy(buf, k, base, target):
        return pltpu.make_async_remote_copy(
            src_ref=buf.at[0],
            dst_ref=buf.at[k],
            send_sem=red_send.at[base + k],
            recv_sem=red_recv.at[base + k],
            device_id=target,
            device_id_type=MESH,
        )

    first_copies = [reduce_copy(red1, k, 0, peer1(k)) for k in range(1, lower)]
    for item in first_copies:
        item.start()

    receive(2, ext)

    def load_p(i, carry):
        put_transform(tp, i, [ext[PR + c, i] for c in range(3)])
        return carry

    lax.fori_loop(4, 13, load_p, 0)

    for item in first_copies:
        item.wait_recv()
    total = red1[0]
    for k in range(1, lower):
        total = total + red1[k]
    red2[0] = total
    second_copies = [reduce_copy(red2, k, lower, peer2(k)) for k in range(1, upper)]
    for item in second_copies:
        item.start()

    for c in range(3):
        def clear_sp(i, carry):
            sp[c, i] = jnp.zeros((L, NZ), jnp.float32)
            return carry
        lax.fori_loop(2, 14, clear_sp, 0)

    def energies(i, carry):
        force = stress(modes(tp, i, own))
        scale = factor[i, own, :]
        for k, held in enumerate((tu, td, tq)):
            sp[k, i, own, :] = scale * dot_modes(modes(held, i, own), force)
        return carry

    lax.fori_loop(W, W + N, energies, 0)
    pack(3, sp)
    send(3)
    receive(3, sp)

    for item in second_copies:
        item.wait_recv()
    total = red2[0]
    for k in range(1, upper):
        total = total + red2[k]
    rz, dw, wq, qv = [jnp.sum(total[k:k + 1, :], axis=1, keepdims=True) for k in range(4)]
    alpha = rz / dw
    after = alpha * alpha * wq - rz
    grow = 1.0 + after / rz
    curve = grow * grow * dw - 2.0 * alpha * grow * wq + alpha * alpha * qv
    beyond = after / curve
    coef_d = alpha + beyond * grow
    coef_q = -beyond * alpha

    def join(i, carry):
        mask[i] = sp[0, i] + coef_d * sp[1, i] + coef_q * sp[2, i]
        return carry

    lax.fori_loop(2, 14, join, 0)

    def result(i, carry):
        row = W + i
        value = filter_row([mask[row + d] for d in range(-2, 3)])
        mine = (1.0 - ext[PAS, row]) * value
        sens[i] = mine[own]
        for c in range(3):
            adjoint[c, i] = (ext[U + c, row, own, :] + coef_d * res_z[c, row, own, :]
                             + coef_q * q[c, row, own, :])
        return carry

    lax.fori_loop(0, N, result, 0)
    for msg in range(4):
        finish(msg)
    for item in first_copies + second_copies:
        item.wait_send()


def local(size_x, size_y, *arrays):
    f32 = jnp.float32
    upper = size_x // 4 * size_y
    scratch = [pltpu.VMEM(stage_shape(*stage), f32) for stage in STAGES]
    scratch += [pltpu.VMEM(route_shape(*route), f32) for route in ROUTES]
    plain = pltpu.VMEM((L, L, NZ), f32)
    three = pltpu.VMEM((3, L, L, NZ), f32)
    twelve = pltpu.VMEM((12, L, L, NZ), f32)
    scratch += [twelve, plain, plain, plain, plain, plain, plain, three, three, plain]
    scratch += [twelve] * 5 + [three]
    scratch += [
        pltpu.VMEM((4, 8, 128), f32),
        pltpu.VMEM((upper, 8, 128), f32),
        pltpu.VMEM((3, L, NZ), f32),
        pltpu.SemaphoreType.DMA((len(ROUTES),)),
        pltpu.SemaphoreType.DMA((len(ROUTES),)),
        pltpu.SemaphoreType.DMA((4 + upper,)),
        pltpu.SemaphoreType.DMA((4 + upper,)),
    ]
    vmem = pl.BlockSpec(memory_space=pltpu.VMEM)
    return pl.pallas_call(
        lambda *refs: kernel(size_x, size_y, *refs),
        out_shape=(
            jax.ShapeDtypeStruct((N, N, NZ), f32),
            jax.ShapeDtypeStruct((3, N, N, NZ), f32),
        ),
        in_specs=[vmem] * 7,
        out_specs=(vmem, vmem),
        scratch_shapes=scratch,
        compiler_params=pltpu.CompilerParams(
            collective_id=0, has_side_effects=True, vmem_limit_bytes=48 * 1024 * 1024
        ),
    )(*arrays)


def solution(mesh):
    grid = P("gx", "gy", None)
    field = P(None, "gx", "gy", None)
    size_x, size_y = mesh.shape["gx"], mesh.shape["gy"]
    return jax.shard_map(
        lambda *arrays: local(size_x, size_y, *arrays),
        mesh=mesh,
        in_specs=(grid, grid, grid, grid, field, field, field),
        out_specs=(grid, field),
        check_vma=False,
    )
```

time: 310 us -> 39.4 us (0.13); the launches traced: 306 us -> 39 us
  blocking collectives: 125 us -> 0 us
  starting transfers between devices: 71.6 us -> 0 us
  local copies, waits for them, and re-layouts: 56.7 us -> 7.44 us
  Pallas kernels: 0 us -> 30.9 us
  other arithmetic: 25.3 us -> 0 us
  waiting for transfers between devices: 11 us -> 0 us
  matrix products: 10.5 us -> 0 us
  between operations: 6.45 us -> 0.66 us
    psum x3 -> x0, blocking collectives: 125 us -> none  [the longest x2 83.1 us: inner_rz(): return lax.psum(jnp.sum(first * second), ('gx', 'gy'))]
    ppermute x26 -> x0, starting transfers between devices: 71.6 us -> none  [the longest x10 30.7 us: with_halo(): after = lax.ppermute(first, axis, down)]
    pallas_call x0 -> x1, Pallas kernels: none -> 30.9 us  [local(): pl.pallas_call(lambda *refs: kernel(size_x, size_y, *refs), out_shape=(ja...]
    unnamed x206 -> x16, local copies, waits for them, and re-layouts: 24.7 us -> 7.44 us
    concatenate x5 -> x0, local copies, waits for them, and re-layouts: 13.7 us -> none  [gather_corners(): jnp.concatenate([corner_field(padded, corner, count_x, count_y, low) for...]
    reshape x6 -> x0, local copies, waits for them, and re-layouts: 11.7 us -> none  [the longest x3 6.37 us: multiply_table(): flat = stacked.reshape(24, -1)]
    ppermute x26 -> x0, waiting for transfers between devices: 11 us -> none  [the longest x10 10.7 us: with_halo(): after = lax.ppermute(first, axis, down)]
    dot_general x4 -> x0, matrix products: 10.5 us -> none  [multiply_table(): jnp.dot(table, flat, precision=HIGH, preferred_element_type=jnp.float32)]
  transfers between devices with their start and end apart: 26 -> 0, of which waited for: 8 -> 0; matrix products, arithmetic and copies ran while one was open for 10% -> 0% of each run, Pallas kernels for 0% -> 0%
where the time goes in v1:
time: 39.4 us; the launch traced here: 39 us
  Pallas kernels  30.9 us (78%)
  local copies, waits for them, and re-layouts  7.44 us (19%)
  between operations  0.66 us (2%)
    pallas_call x1, Pallas kernels, local(): pl.pallas_call(lambda *refs: kernel(size_x, size_y, *refs), out_shape=(ja...  30.9 us
    unnamed x16, local copies, waits for them, and re-layouts  7.44 us

profile of v1, /device:TPU:5, one launch (start us, length us, event | category | flops | bytes accessed | tf_op | source)
XLA Modules:
  0.0 39.0 jit_solution(9075220671886426684)
XLA Ops:
  0.6 0.0 copy-start
  0.6 0.9 %copy-done = f32[3,8,8,256]{3,2,1,0:T(8,128)S(1)} copy-done((f32[3,8,8,256]{3,2,1,0:T(8,128)S(1)}, f32[3,8,8,256]{3,2,1,0:T(8,128)}, u32[]{:S(2)}) %copy-start) | copy-done | bytes 196632
  1.6 0.0 copy-start.1
  1.6 0.9 %copy-done.1 = f32[3,8,8,256]{3,2,1,0:T(8,128)S(1)} copy-done((f32[3,8,8,256]{3,2,1,0:T(8,128)S(1)}, f32[3,8,8,256]{3,2,1,0:T(8,128)}, u32[]{:S(2)}) %copy-start.1) | copy-done | bytes 196632
  2.5 0.0 copy-start.2
  2.5 0.9 %copy-done.2 = f32[3,8,8,256]{3,2,1,0:T(8,128)S(1)} copy-done((f32[3,8,8,256]{3,2,1,0:T(8,128)S(1)}, f32[3,8,8,256]{3,2,1,0:T(8,128)}, u32[]{:S(2)}) %copy-start.2) | copy-done | bytes 196632
  3.4 0.0 copy-start.3
  3.4 0.8 %copy-done.3 = f32[8,8,256]{2,1,0:T(8,128)S(1)} copy-done((f32[8,8,256]{2,1,0:T(8,128)S(1)}, f32[8,8,256]{2,1,0:T(8,128)}, u32[]{:S(2)}) %copy-start.3) | copy-done | bytes 65560
  4.3 0.0 copy-start.4
  4.3 0.8 %copy-done.4 = s32[8,8,256]{2,1,0:T(8,128)S(1)} copy-done((s32[8,8,256]{2,1,0:T(8,128)S(1)}, s32[8,8,256]{2,1,0:T(8,128)}, u32[]{:S(2)}) %copy-start.4) | copy-done | bytes 65560
  5.1 0.0 copy-start.5
  5.1 0.8 %copy-done.5 = s32[8,8,256]{2,1,0:T(8,128)S(1)} copy-done((s32[8,8,256]{2,1,0:T(8,128)S(1)}, s32[8,8,256]{2,1,0:T(8,128)}, u32[]{:S(2)}) %copy-start.5) | copy-done | bytes 65560
  5.9 0.0 copy-start.6
  5.9 0.8 %copy-done.6 = s32[8,8,256]{2,1,0:T(8,128)S(1)} copy-done((s32[8,8,256]{2,1,0:T(8,128)S(1)}, s32[8,8,256]{2,1,0:T(8,128)}, u32[]{:S(2)}) %copy-start.6) | copy-done | bytes 65560
  6.8 30.9 %shard_map.86 = (f32[8,8,256]{2,1,0:T(8,128)S(1)}, f32[3,8,8,256]{3,2,1,0:T(8,128)S(1)}) custom-call(f32[8,8,256]{2,1,0:T(8,128)S(1)} %copy-done.3, s32[8,8,256]{2,1,0:T(8,128)S(1)} %copy-done.4, s32[8,8,256]{2,1,0:T(8,128)S(1)} %copy-done.5, s32[8,8,256]{2,1,0:T(8,128)S(1)} %copy-done.6, f32[3,8,8,256]{3,2,1,0:T(8,128)S(1)} %copy-done, ...), custom_call_target="tpu_custom_call" | custom-call | tf_op jit(solution)/shard_map/pallas_call | solution.py:600
  37.7 0.6 %copy.11 = f32[8,8,256]{2,1,0:T(8,128)} copy(f32[8,8,256]{2,1,0:T(8,128)S(1)} %get-tuple-element.4) | data formatting | bytes 131072
  38.3 0.7 %copy.12 = f32[3,8,8,256]{3,2,1,0:T(8,128)} copy(f32[3,8,8,256]{3,2,1,0:T(8,128)S(1)} %get-tuple-element.5) | data formatting | bytes 393216
Async XLA Ops:
  0.6 0.9 %copy-start = (f32[3,8,8,256]{3,2,1,0:T(8,128)S(1)}, f32[3,8,8,256]{3,2,1,0:T(8,128)}, u32[]{:S(2)}) copy-start(f32[3,8,8,256]{3,2,1,0:T(8,128)} %refs_4_.1) | copy-start | bytes 589828
  1.6 0.9 %copy-start.1 = (f32[3,8,8,256]{3,2,1,0:T(8,128)S(1)}, f32[3,8,8,256]{3,2,1,0:T(8,128)}, u32[]{:S(2)}) copy-start(f32[3,8,8,256]{3,2,1,0:T(8,128)} %refs_5_.1) | copy-start | bytes 589828
  2.5 0.9 %copy-start.2 = (f32[3,8,8,256]{3,2,1,0:T(8,128)S(1)}, f32[3,8,8,256]{3,2,1,0:T(8,128)}, u32[]{:S(2)}) copy-start(f32[3,8,8,256]{3,2,1,0:T(8,128)} %refs_6_.1) | copy-start | bytes 589828
  3.4 0.8 %copy-start.3 = (f32[8,8,256]{2,1,0:T(8,128)S(1)}, f32[8,8,256]{2,1,0:T(8,128)}, u32[]{:S(2)}) copy-start(f32[8,8,256]{2,1,0:T(8,128)} %refs_0_.1) | copy-start | bytes 196612
  4.3 0.8 %copy-start.4 = (s32[8,8,256]{2,1,0:T(8,128)S(1)}, s32[8,8,256]{2,1,0:T(8,128)}, u32[]{:S(2)}) copy-start(s32[8,8,256]{2,1,0:T(8,128)} %refs_1_.1) | copy-start | bytes 196612
  5.1 0.8 %copy-start.5 = (s32[8,8,256]{2,1,0:T(8,128)S(1)}, s32[8,8,256]{2,1,0:T(8,128)}, u32[]{:S(2)}) copy-start(s32[8,8,256]{2,1,0:T(8,128)} %refs_2_.1) | copy-start | bytes 196612
  5.9 0.8 %copy-start.6 = (s32[8,8,256]{2,1,0:T(8,128)S(1)}, s32[8,8,256]{2,1,0:T(8,128)}, u32[]{:S(2)}) copy-start(s32[8,8,256]{2,1,0:T(8,128)} %refs_3_.1) | copy-start | bytes 196612

commit v2 on v1

--- a/solution.py
+++ b/solution.py
@@ -247,12 +247,16 @@
 
 def kernel(size_x, size_y, *refs):
     inputs, refs = refs[:7], refs[7:]
-    density, passive, fixed, load_nodes, port, guess, primal = inputs
     (sens, adjoint), refs = refs[:2], refs[2:]
+    held, refs = refs[:7], refs[7:]
+    density, passive, fixed, load_nodes, port, guess, primal = held
     stages, refs = dict(zip(STAGES, refs)), refs[len(STAGES):]
     lands, refs = dict(zip(ROUTES, refs)), refs[len(ROUTES):]
     (ext, mask, weight, phys, slope, stiff, factor, res_z, q, inv, tu, td, tq, tp, work, sp,
-     red1, red2, acc, send_sem, recv_sem, red_send, red_recv) = refs
+     red1, red2, acc, send_sem, recv_sem, red_send, red_recv, in_sem) = refs
+    loads = [pltpu.make_async_copy(a, b, in_sem.at[k]) for k, (a, b) in enumerate(zip(inputs, held))]
+    for item in loads:
+        item.start()
     gx, gy = lax.axis_index("gx"), lax.axis_index("gy")
     lower = 4
     upper = size_x // lower * size_y
@@ -290,12 +294,33 @@
     for k in range(1, upper):
         pl.semaphore_signal(barrier, inc=1, device_id=peer2(k), device_id_type=MESH)
 
+    sub = lax.broadcasted_iota(jnp.int32, (L, NZ), 0)
+    at_y = gy * N - W + sub
+    inside_y = ((at_y >= 0) & (at_y < size_y * N)).astype(jnp.float32)
+    owned = ((sub >= W) & (sub < W + N)).astype(jnp.float32)
+
+    def inside_x(i):
+        at_x = gx * N - W + i
+        return ((at_x >= 0) & (at_x < size_x * N)).astype(jnp.float32)
+
+    def weigh(i, carry):
+        total = filter_row([inside_x(i + d) * inside_y for d in range(-2, 3)])
+        weight[i] = 1.0 / jnp.where(total > 0.0, total, 1.0)
+        return carry
+
+    lax.fori_loop(2, 14, weigh, 0)
+
     own = slice(W, W + N)
-    for f in range(FIELDS):
-        def clear(i, carry):
+    def clear(i, carry):
+        for f in range(FIELDS):
             ext[f, i] = jnp.zeros((L, NZ), jnp.float32)
-            return carry
-        lax.fori_loop(0, L, clear, 0)
+        for c in range(3):
+            sp[c, i] = jnp.zeros((L, NZ), jnp.float32)
+        return carry
+
+    lax.fori_loop(0, L, clear, 0)
+    for item in loads:
+        item.wait()
 
     def fill(i, carry):
         free = (1 - fixed[i]).astype(jnp.float32)
@@ -390,22 +415,6 @@
     pack(2, ext)
     send(2)
 
-    sub = lax.broadcasted_iota(jnp.int32, (L, NZ), 0)
-    at_y = gy * N - W + sub
-    inside_y = ((at_y >= 0) & (at_y < size_y * N)).astype(jnp.float32)
-    owned = ((sub >= W) & (sub < W + N)).astype(jnp.float32)
-
-    def inside_x(i):
-        at_x = gx * N - W + i
-        return ((at_x >= 0) & (at_x < size_x * N)).astype(jnp.float32)
-
-    def weigh(i, carry):
-        total = filter_row([inside_x(i + d) * inside_y for d in range(-2, 3)])
-        weight[i] = 1.0 / jnp.where(total > 0.0, total, 1.0)
-        return carry
-
-    lax.fori_loop(2, 14, weigh, 0)
-
     receive(0, ext)
     denom = 2.0 * math.tanh(BETA * ETA)
 
@@ -522,12 +531,6 @@
     for item in second_copies:
         item.start()
 
-    for c in range(3):
-        def clear_sp(i, carry):
-            sp[c, i] = jnp.zeros((L, NZ), jnp.float32)
-            return carry
-        lax.fori_loop(2, 14, clear_sp, 0)
-
     def energies(i, carry):
         force = stress(modes(tp, i, own))
         scale = factor[i, own, :]
@@ -580,7 +583,8 @@
 def local(size_x, size_y, *arrays):
     f32 = jnp.float32
     upper = size_x // 4 * size_y
-    scratch = [pltpu.VMEM(stage_shape(*stage), f32) for stage in STAGES]
+    scratch = [pltpu.VMEM(array.shape, array.dtype) for array in arrays]
+    scratch += [pltpu.VMEM(stage_shape(*stage), f32) for stage in STAGES]
     scratch += [pltpu.VMEM(route_shape(*route), f32) for route in ROUTES]
     plain = pltpu.VMEM((L, L, NZ), f32)
     three = pltpu.VMEM((3, L, L, NZ), f32)
@@ -595,6 +599,7 @@
         pltpu.SemaphoreType.DMA((len(ROUTES),)),
         pltpu.SemaphoreType.DMA((4 + upper,)),
         pltpu.SemaphoreType.DMA((4 + upper,)),
+        pltpu.SemaphoreType.DMA((7,)),
     ]
     vmem = pl.BlockSpec(memory_space=pltpu.VMEM)
     return pl.pallas_call(
@@ -603,11 +608,11 @@
             jax.ShapeDtypeStruct((N, N, NZ), f32),
             jax.ShapeDtypeStruct((3, N, N, NZ), f32),
         ),
-        in_specs=[vmem] * 7,
+        in_specs=[pl.BlockSpec(memory_space=pltpu.HBM)] * 7,
         out_specs=(vmem, vmem),
         scratch_shapes=scratch,
         compiler_params=pltpu.CompilerParams(
-            collective_id=0, has_side_effects=True, vmem_limit_bytes=48 * 1024 * 1024
+            collective_id=0, has_side_effects=True, vmem_limit_bytes=65000 * 1024
         ),
     )(*arrays)
 

time: 39.4 us -> 35.5 us (0.901)
  local copies, waits for them, and re-layouts: 7.44 us -> 3.09 us
  Pallas kernels: 30.9 us -> 31.6 us
    unnamed x16 -> x2, local copies, waits for them, and re-layouts: 7.44 us -> 3.09 us
    pallas_call x1, Pallas kernels: 30.9 us -> 31.6 us  [local(): pl.pallas_call(lambda *refs: kernel(size_x, size_y, *refs), out_shape=(ja...]
where the time goes in v2:
time: 35.5 us; the launch traced here: 35.3 us
  Pallas kernels  31.6 us (89%)
  local copies, waits for them, and re-layouts  3.09 us (9%)
  between operations  0.64 us (2%)
    pallas_call x1, Pallas kernels, local(): pl.pallas_call(lambda *refs: kernel(size_x, size_y, *refs), out_shape=(ja...  31.6 us
    unnamed x2, local copies, waits for them, and re-layouts  3.09 us

profile of v2, /device:TPU:5, one launch (start us, length us, event | category | flops | bytes accessed | tf_op | source)
XLA Modules:
  0.0 35.3 jit_solution(130441443547964145)
XLA Ops:
  0.6 31.6 %shard_map.86 = (f32[8,8,256]{2,1,0:T(8,128)}, f32[3,8,8,256]{3,2,1,0:T(8,128)}) custom-call(f32[8,8,256]{2,1,0:T(8,128)} %refs_0_.1, s32[8,8,256]{2,1,0:T(8,128)} %refs_1_.1, s32[8,8,256]{2,1,0:T(8,128)} %refs_2_.1, s32[8,8,256]{2,1,0:T(8,128)} %refs_3_.1, f32[3,8,8,256]{3,2,1,0:T(8,128)} %refs_4_.1, f32[3,8,8,256]{3,2,1,0:T(8,128)} %refs_5_.1, ...), custom_call_target="tpu_custom_call" | custom-call | tf_op jit(solution)/shard_map/pallas_call | solution.py:605
  32.3 1.5 %copy.11 = f32[8,8,256]{2,1,0:T(8,128)} copy(f32[8,8,256]{2,1,0:T(8,128)} %get-tuple-element.4) | data formatting | bytes 131072
  33.7 1.6 %copy.12 = f32[3,8,8,256]{3,2,1,0:T(8,128)} copy(f32[3,8,8,256]{3,2,1,0:T(8,128)} %get-tuple-element.5) | data formatting | bytes 393216

commit v3 on v2

--- a/solution.py
+++ b/solution.py
@@ -119,7 +119,14 @@
     return found
 
 
-ROUTES = routes()
+RELAYED = (0, 1, 2)
+
+
+def is_relay(route):
+    return route[0] in RELAYED and route[1] != 0 and route[2] != 0
+
+
+ROUTES = sorted(routes(), key=lambda r: (r[0], r[1] != 0, r[1] != 0 and r[2] != 0))
 STAGES = [(msg, axis, way) for (msg, way) in MSG for axis in (0, 1)]
 
 
@@ -360,19 +367,22 @@
             source = stages[msg, 1, dy]
         else:
             first, count = DIAG_ROWS[msg, dx]
-            source = stages[msg, 1, dy].at[first:first + count]
+            if msg in RELAYED:
+                source = lands[msg, 0, dy].at[first:first + count]
+            else:
+                source = stages[msg, 1, dy].at[first:first + count]
         return pltpu.make_async_remote_copy(
             src_ref=source,
             dst_ref=lands[route],
             send_sem=send_sem.at[at],
             recv_sem=recv_sem.at[at],
-            device_id=(gx + dx, gy + dy),
+            device_id=(gx + dx, gy if dx and msg in RELAYED else gy + dy),
             device_id_type=MESH,
         )
 
     def send(msg):
         for route in ROUTES:
-            if route[0] == msg:
+            if route[0] == msg and not is_relay(route):
                 @pl.when(there(route[1], route[2]))
                 def _():
                     copy(route).start()
@@ -387,6 +397,12 @@
             def _():
                 copy(route).wait_recv()
                 land = lands[route]
+                if dx == 0:
+                    for other in ROUTES:
+                        if other[0] == msg and other[2] == dy and is_relay(other):
+                            @pl.when(there(other[1], 0))
+                            def _():
+                                copy(other).start()
                 at = 0
                 for f, first, count in MSG[msg, dy if dy else dx]:
                     begin = W + first
@@ -403,7 +419,9 @@
     def finish(msg):
         for route in ROUTES:
             if route[0] == msg:
-                @pl.when(there(route[1], route[2]))
+                _, dx, dy = route
+
+                @pl.when(there(dx, 0) & there(0, -dy) if is_relay(route) else there(dx, dy))
                 def _():
                     copy(route).wait_send()
 

time: 35.5 us -> 38.8 us (1.093)
  the two profiles are of different devices: /device:TPU:5 before, /device:TPU:0 now
where the time goes in v3:
time: 38.8 us; the launch traced here: 38.6 us
  Pallas kernels  34.8 us (90%)
  local copies, waits for them, and re-layouts  3.09 us (8%)
  between operations  0.64 us (2%)
    pallas_call x1, Pallas kernels, local(): pl.pallas_call(lambda *refs: kernel(size_x, size_y, *refs), out_shape=(ja...  34.8 us
    unnamed x2, local copies, waits for them, and re-layouts  3.09 us

profile of v3, /device:TPU:0, one launch (start us, length us, event | category | flops | bytes accessed | tf_op | source)
XLA Modules:
  0.0 38.6 jit_solution(275157599709086916)
XLA Ops:
  0.6 34.8 %shard_map.86 = (f32[8,8,256]{2,1,0:T(8,128)}, f32[3,8,8,256]{3,2,1,0:T(8,128)}) custom-call(f32[8,8,256]{2,1,0:T(8,128)} %refs_0_.1, s32[8,8,256]{2,1,0:T(8,128)} %refs_1_.1, s32[8,8,256]{2,1,0:T(8,128)} %refs_2_.1, s32[8,8,256]{2,1,0:T(8,128)} %refs_3_.1, f32[3,8,8,256]{3,2,1,0:T(8,128)} %refs_4_.1, f32[3,8,8,256]{3,2,1,0:T(8,128)} %refs_5_.1, ...), custom_call_target="tpu_custom_call" | custom-call | tf_op jit(solution)/shard_map/pallas_call | solution.py:623
  35.5 1.5 %copy.11 = f32[8,8,256]{2,1,0:T(8,128)} copy(f32[8,8,256]{2,1,0:T(8,128)} %get-tuple-element.4) | data formatting | bytes 131072
  36.9 1.6 %copy.12 = f32[3,8,8,256]{3,2,1,0:T(8,128)} copy(f32[3,8,8,256]{3,2,1,0:T(8,128)} %get-tuple-element.5) | data formatting | bytes 393216

commit v4 on v2

--- a/solution.py
+++ b/solution.py
@@ -521,6 +521,17 @@
 
     lax.fori_loop(4, 13, load_p, 0)
 
+    def energies(i, carry):
+        force = stress(modes(tp, i, own))
+        scale = factor[i, own, :]
+        for k, held in enumerate((tu, td, tq)):
+            sp[k, i, own, :] = scale * dot_modes(modes(held, i, own), force)
+        return carry
+
+    lax.fori_loop(W, W + N, energies, 0)
+    pack(3, sp)
+    send(3)
+
     for item in first_copies:
         item.wait_recv()
     total = red1[0]
@@ -531,16 +542,6 @@
     for item in second_copies:
         item.start()
 
-    def energies(i, carry):
-        force = stress(modes(tp, i, own))
-        scale = factor[i, own, :]
-        for k, held in enumerate((tu, td, tq)):
-            sp[k, i, own, :] = scale * dot_modes(modes(held, i, own), force)
-        return carry
-
-    lax.fori_loop(W, W + N, energies, 0)
-    pack(3, sp)
-    send(3)
     receive(3, sp)
 
     for item in second_copies:

time: 35.5 us -> 35.7 us (level)
  the two profiles are of different devices: /device:TPU:5 before, /device:TPU:0 now
where the time goes in v4:
time: 35.7 us; the launch traced here: 35.5 us
  Pallas kernels  31.8 us (89%)
  local copies, waits for them, and re-layouts  3.09 us (9%)
  between operations  0.64 us (2%)
    pallas_call x1, Pallas kernels, local(): pl.pallas_call(lambda *refs: kernel(size_x, size_y, *refs), out_shape=(ja...  31.8 us
    unnamed x2, local copies, waits for them, and re-layouts  3.09 us

profile of v4, /device:TPU:0, one launch (start us, length us, event | category | flops | bytes accessed | tf_op | source)
XLA Modules:
  0.0 35.5 jit_solution(3799431444592877060)
XLA Ops:
  0.6 31.8 %shard_map.86 = (f32[8,8,256]{2,1,0:T(8,128)}, f32[3,8,8,256]{3,2,1,0:T(8,128)}) custom-call(f32[8,8,256]{2,1,0:T(8,128)} %refs_0_.1, s32[8,8,256]{2,1,0:T(8,128)} %refs_1_.1, s32[8,8,256]{2,1,0:T(8,128)} %refs_2_.1, s32[8,8,256]{2,1,0:T(8,128)} %refs_3_.1, f32[3,8,8,256]{3,2,1,0:T(8,128)} %refs_4_.1, f32[3,8,8,256]{3,2,1,0:T(8,128)} %refs_5_.1, ...), custom_call_target="tpu_custom_call" | custom-call | tf_op jit(solution)/shard_map/pallas_call | solution.py:606
  32.4 1.5 %copy.11 = f32[8,8,256]{2,1,0:T(8,128)} copy(f32[8,8,256]{2,1,0:T(8,128)} %get-tuple-element.4) | data formatting | bytes 131072
  33.9 1.6 %copy.12 = f32[3,8,8,256]{3,2,1,0:T(8,128)} copy(f32[3,8,8,256]{3,2,1,0:T(8,128)} %get-tuple-element.5) | data formatting | bytes 393216

commit v5 on v2

--- a/solution.py
+++ b/solution.py
@@ -294,22 +294,6 @@
     for k in range(1, upper):
         pl.semaphore_signal(barrier, inc=1, device_id=peer2(k), device_id_type=MESH)
 
-    sub = lax.broadcasted_iota(jnp.int32, (L, NZ), 0)
-    at_y = gy * N - W + sub
-    inside_y = ((at_y >= 0) & (at_y < size_y * N)).astype(jnp.float32)
-    owned = ((sub >= W) & (sub < W + N)).astype(jnp.float32)
-
-    def inside_x(i):
-        at_x = gx * N - W + i
-        return ((at_x >= 0) & (at_x < size_x * N)).astype(jnp.float32)
-
-    def weigh(i, carry):
-        total = filter_row([inside_x(i + d) * inside_y for d in range(-2, 3)])
-        weight[i] = 1.0 / jnp.where(total > 0.0, total, 1.0)
-        return carry
-
-    lax.fori_loop(2, 14, weigh, 0)
-
     own = slice(W, W + N)
     def clear(i, carry):
         for f in range(FIELDS):
@@ -414,6 +398,22 @@
     send(1)
     pack(2, ext)
     send(2)
+
+    sub = lax.broadcasted_iota(jnp.int32, (L, NZ), 0)
+    at_y = gy * N - W + sub
+    inside_y = ((at_y >= 0) & (at_y < size_y * N)).astype(jnp.float32)
+    owned = ((sub >= W) & (sub < W + N)).astype(jnp.float32)
+
+    def inside_x(i):
+        at_x = gx * N - W + i
+        return ((at_x >= 0) & (at_x < size_x * N)).astype(jnp.float32)
+
+    def weigh(i, carry):
+        total = filter_row([inside_x(i + d) * inside_y for d in range(-2, 3)])
+        weight[i] = 1.0 / jnp.where(total > 0.0, total, 1.0)
+        return carry
+
+    lax.fori_loop(2, 14, weigh, 0)
 
     receive(0, ext)
     denom = 2.0 * math.tanh(BETA * ETA)

time: 35.5 us -> 35.6 us (level)
  no operation moved by 1% of the time
where the time goes in v5:
time: 35.6 us; the launch traced here: 35.4 us
  Pallas kernels  31.6 us (89%)
  local copies, waits for them, and re-layouts  3.09 us (9%)
  between operations  0.64 us (2%)
    pallas_call x1, Pallas kernels, local(): pl.pallas_call(lambda *refs: kernel(size_x, size_y, *refs), out_shape=(ja...  31.6 us
    unnamed x2, local copies, waits for them, and re-layouts  3.09 us

profile of v5, /device:TPU:5, one launch (start us, length us, event | category | flops | bytes accessed | tf_op | source)
XLA Modules:
  0.0 35.4 jit_solution(10717632549870890549)
XLA Ops:
  0.6 31.6 %shard_map.86 = (f32[8,8,256]{2,1,0:T(8,128)}, f32[3,8,8,256]{3,2,1,0:T(8,128)}) custom-call(f32[8,8,256]{2,1,0:T(8,128)} %refs_0_.1, s32[8,8,256]{2,1,0:T(8,128)} %refs_1_.1, s32[8,8,256]{2,1,0:T(8,128)} %refs_2_.1, s32[8,8,256]{2,1,0:T(8,128)} %refs_3_.1, f32[3,8,8,256]{3,2,1,0:T(8,128)} %refs_4_.1, f32[3,8,8,256]{3,2,1,0:T(8,128)} %refs_5_.1, ...), custom_call_target="tpu_custom_call" | custom-call | tf_op jit(solution)/shard_map/pallas_call | solution.py:605
  32.3 1.5 %copy.11 = f32[8,8,256]{2,1,0:T(8,128)} copy(f32[8,8,256]{2,1,0:T(8,128)} %get-tuple-element.4) | data formatting | bytes 131072
  33.7 1.6 %copy.12 = f32[3,8,8,256]{3,2,1,0:T(8,128)} copy(f32[3,8,8,256]{3,2,1,0:T(8,128)} %get-tuple-element.5) | data formatting | bytes 393216
